TPU v7x, 128 devices: a whole 4x4x4 slice. The times are simulated.
128 devices in a mesh: ctx: 8 (over z, x_hi), tp: 16 (over y, x_lo, core).
Axes of the slice: x: 4 (x_hi: 2, x_lo: 2; x = x_hi * 2 + x_lo), y: 4, z: 4, core: 2. Of those that a mesh axis runs over, the one named last changes fastest.
Arguments:
- prompt_queries: bfloat16 [4096, 16384], P('ctx', 'tp'), may hold values from -10 to 10
- prompt_keys: bfloat16 [4096, 1024], P('ctx', 'tp'), may hold values from -10 to 10
- prompt_values: bfloat16 [4096, 1024], P('ctx', 'tp'), may hold values from -6 to 6
- block_slot: int32 [32], replicated, may hold values from 0 to 31, each once
- decode_queries: bfloat16 [512, 16384], P('ctx', 'tp'), may hold values from -10 to 10
- new_keys: bfloat16 [512, 1024], P('ctx', 'tp'), may hold values from -6 to 6
- new_values: bfloat16 [512, 1024], P('ctx', 'tp'), may hold values from -6 to 6
- key_pool: bfloat16 [2048, 128, 1024], P(('ctx', 'tp')), may hold values from -10 to 10
- value_pool: bfloat16 [2048, 128, 1024], P(('ctx', 'tp')), may hold values from -6 to 6
- slot_map: int32 [512, 4], P(('ctx', 'tp')), may hold values from 0 to 15, as said below
- cache_lengths: int32 [512], P(('ctx', 'tp')), may hold values from 2 to 512, as said below
Outputs:
- prompt_out: bfloat16 [4096, 16384], P('ctx', 'tp')
- relaid_keys: bfloat16 [32, 128, 1024], P('ctx', None, 'tp')
- relaid_values: bfloat16 [32, 128, 1024], P('ctx', None, 'tp')
- decode_out: bfloat16 [512, 16384], P('ctx', 'tp')
Inputs may be any that keep to these rules, and one draw needn't show every extreme that they name: `slot_map`: within the 4 rows of one device the 16 entries are all different. `cache_lengths`: on every device some row has exactly 512 cached tokens.
All inputs are finite; a program needn't handle non-finite values.
Results may differ from a plain program's by a relative error of at most 0.006.
Values may be sent and summed in bfloat16 or wider, within the bound.
A program may use at most 128 MiB of HBM per device.

v0:
```python
import functools
import math

import jax
import jax.numpy as jnp
from jax import lax
from jax.experimental import pallas as pl
from jax.experimental.pallas import tpu as pltpu
from jax.sharding import PartitionSpec as P

HEAD = 128
PAGE = 128
CTX = 8
TP = 16
SEQ = 512
HEADS = 8
GROUPS = 8
ROWS = 4
SPAN = 2048
HELP = 2
MSG = 48
F32 = jnp.float32
BF16 = jnp.bfloat16
MESH = pl.DeviceIdType.MESH
LOW = -1e30
SCALE = math.log2(math.e) / math.sqrt(HEAD)


def split_scaled(x):
    x = x.astype(F32) * SCALE
    high = x.astype(BF16)
    low = (x - high.astype(F32)).astype(BF16)
    return jnp.concatenate([high, low], axis=1)


def kernel(
    pq_ref, kt_in, vt_in, dq_in, nk_in, nv_in, kp_ref, vp_ref, slots_ref, lens_ref, place_ref,
    out_ref, rk_ref, rv_ref, dout_ref,
    pq, qs, kv, vn, m_s, l_s, acc_s, kpool, vpool, bias, dsend, drecv, rsend, rrecv, lent, repaid, returned, s_even, s_odd, p_even, p_odd, f_even, f_odd,
    kt_ref, vt_ref, dq_ref, nk_ref, nv_ref,
    local_sem, kv_ssem, kv_rsem, fw_ssem, fw_rsem, d_ssem, d_rsem, r_ssem, r_rsem, h_ssem, h_rsem, b_ssem, b_rsem,
):
    me = lax.axis_index("ctx")
    tp = lax.axis_index("tp")
    core = tp % 2
    mate = tp + 1 - 2 * core
    donor = me >= CTX - 2
    helper = me < 2
    partner = me ^ 6

    barrier = pltpu.get_barrier_semaphore()
    for d in range(1, CTX):
        pl.semaphore_signal(barrier, inc=1, device_id=((me + d) % CTX, tp), device_id_type=MESH)
    for d in range(1, TP):
        pl.semaphore_signal(barrier, inc=1, device_id=(me, (tp + d) % TP), device_id_type=MESH)

    pairs = ((dq_in, dq_ref), (nk_in, nk_ref), (nv_in, nv_ref), (kt_in, kt_ref), (vt_in, vt_ref))
    small = [
        pltpu.make_async_copy(given, held, local_sem.at[3 + i])
        for i, (given, held) in enumerate(pairs)
    ]
    for copy in small:
        copy.start()
    load_q = pltpu.make_async_copy(pq_ref, pq, local_sem.at[0])
    load_k = pltpu.make_async_copy(kp_ref, kpool, local_sem.at[1])
    load_v = pltpu.make_async_copy(vp_ref, vpool, local_sem.at[2])
    load_q.start()
    load_k.start()
    load_v.start()

    half = pl.ds(pl.multiple_of(core * 64, 64), 64)

    def tokens(block):
        return pl.ds(pl.multiple_of(block * SEQ, SEQ), SEQ)

    for copy in small:
        copy.wait()
    kv[0, half, tokens(me)] = kt_ref[...]
    kv[1, half, tokens(me)] = vt_ref[...]

    sub = lax.broadcasted_iota(jnp.int32, (8, HEAD), 0)
    lane = lax.broadcasted_iota(jnp.int32, (8, HEAD), 1)
    first_rows = sub < 4
    for p in range(4):
        x16 = dq_ref[16 * p : 16 * p + 16, :].astype(F32)
        n16 = jnp.concatenate(
            [nk_ref[16 * p : 16 * p + 16, :], nv_ref[16 * p : 16 * p + 16, :]], axis=1
        ).astype(F32)
        for o in range(2):
            x = x16[8 * o : 8 * o + 8]
            n = n16[8 * o : 8 * o + 8]
            even, odd = [], []
            for i in range(4):
                a = x[:, 2 * i * HEAD : (2 * i + 1) * HEAD]
                b = x[:, (2 * i + 1) * HEAD : (2 * i + 2) * HEAD]
                even.append(jnp.where(first_rows, a, pltpu.roll(b, 4, 0)))
                odd.append(jnp.where(first_rows, pltpu.roll(a, 4, 0), b))
            turned = pltpu.roll(n, 4, 0)
            dsend[4 * p + 2 * o] = jnp.concatenate(even + [n, n], axis=0).astype(BF16)
            dsend[4 * p + 2 * o + 1] = jnp.concatenate(odd + [turned, turned], axis=0).astype(BF16)
    drecv[tp] = dsend[tp]

    pl.semaphore_wait(barrier, CTX + TP - 2)

    def push(block, ctx):
        return pltpu.make_async_remote_copy(
            src_ref=kv.at[:, half, tokens(block)],
            dst_ref=kv.at[:, half, tokens(block)],
            send_sem=kv_ssem.at[ctx],
            recv_sem=kv_rsem.at[block],
            device_id=(ctx, tp),
            device_id_type=MESH,
        )

    def forward(block):
        return pltpu.make_async_remote_copy(
            src_ref=kv.at[:, half, tokens(block)],
            dst_ref=kv.at[:, half, tokens(block)],
            send_sem=fw_ssem.at[block],
            recv_sem=fw_rsem.at[block],
            device_id=(me, mate),
            device_id_type=MESH,
        )

    def ask(other, slot):
        return pltpu.make_async_remote_copy(
            src_ref=dsend.at[other],
            dst_ref=drecv.at[slot],
            send_sem=d_ssem.at[other],
            recv_sem=d_rsem.at[slot],
            device_id=(me, other),
            device_id_type=MESH,
        )

    def answer(other, slot):
        return pltpu.make_async_remote_copy(
            src_ref=rsend.at[other],
            dst_ref=rrecv.at[slot],
            send_sem=r_ssem.at[other],
            recv_sem=r_rsem.at[slot],
            device_id=(me, other),
            device_id_type=MESH,
        )

    def others(do):
        def body(d, carry):
            do((tp + d) % TP)
            return carry

        lax.fori_loop(1, TP, body, 0)

    def needs(ctx, block):
        return block <= jnp.where(ctx < 2, ctx + 6, ctx)

    def lend(i):
        return pltpu.make_async_remote_copy(
            src_ref=pq.at[:, pl.ds((HEADS - HELP + i) * HEAD, HEAD)],
            dst_ref=lent.at[i],
            send_sem=h_ssem.at[i],
            recv_sem=h_rsem.at[i],
            device_id=(partner, tp),
            device_id_type=MESH,
        )

    def give_back(i):
        return pltpu.make_async_remote_copy(
            src_ref=repaid.at[i],
            dst_ref=returned.at[i],
            send_sem=b_ssem.at[i],
            recv_sem=b_rsem.at[i],
            device_id=(partner, tp),
            device_id_type=MESH,
        )

    nearest = (1, 2, 3, 6, 7, 4, 5)
    forward(me).start()
    others(lambda other: ask(other, tp).start())
    load_q.wait()

    for d in nearest:

        @pl.when(needs(me ^ d, me))
        def _(d=d):
            push(me, me ^ d).start()

    @pl.when(donor)
    def _():
        for i in range(HELP):
            lend(i).start()

    for d in nearest:

        @pl.when(jnp.logical_not(needs(me ^ d, me)))
        def _(d=d):
            push(me, me ^ d).start()


    token = lax.broadcasted_iota(jnp.int32, (8, SPAN), 1)
    row = lax.broadcasted_iota(jnp.int32, (8, SPAN), 0) % ROWS
    visible = jnp.zeros((8, SPAN), F32)
    for r in range(ROWS):
        for b in range(4):
            left = jnp.minimum(lens_ref[r] - b * PAGE, PAGE)
            start = slots_ref[r, b] * PAGE
            inside = (token >= start) & (token < start + left) & (row == r)
            visible = jnp.where(inside, 1.0, visible)
    bias[...] = jnp.where(visible > 0.5, 0.0, LOW)

    for h in range(HEADS):
        qs[h] = split_scaled(pq[:, h * HEAD : (h + 1) * HEAD])

    def turn(block):
        vn[tokens(block), :] = kv[1, :, tokens(block)].T

    def unit(h, block, count, diagonal):
        width = count * SEQ
        where = pl.ds(pl.multiple_of(block * SEQ, SEQ), width)
        keys = kv[0, :, where]
        s = jnp.dot(qs[h], jnp.concatenate([keys, keys], axis=0), preferred_element_type=F32)
        if diagonal:
            query = lax.broadcasted_iota(jnp.int32, s.shape, 0)
            key = lax.broadcasted_iota(jnp.int32, s.shape, 1)
            s = jnp.where(key <= query, s, LOW)
        peak = jnp.max(s, axis=1, keepdims=True)
        if diagonal:
            peak = jnp.broadcast_to(peak, (SEQ, HEAD))
        else:
            before = m_s[h]
            peak = jnp.maximum(before, peak)
            factor = jnp.exp2(before - peak)
        m_s[h] = peak
        probs, total = [], None
        for g in range(width // HEAD):
            p = jnp.exp2(s[:, g * HEAD : (g + 1) * HEAD] - peak)
            total = p if total is None else total + p
            probs.append(p.astype(BF16))
        mixed = jnp.dot(jnp.concatenate(probs, axis=1), vn[where, :], preferred_element_type=F32)
        if diagonal:
            l_s[h] = total
            acc_s[h] = mixed
        else:
            l_s[h] = l_s[h] * factor + total
            acc_s[h] = acc_s[h] * factor + mixed

    def heads(first, last, block, count, diagonal=False):
        def body(i, carry):
            unit(2 * i, block, count, diagonal)
            unit(2 * i + 1, block, count, diagonal)
            return carry

        lax.fori_loop(first // 2, last // 2, body, 0)

    def scores(h, where, held):
        s_ref, peak_ref, factor_ref = held
        keys = kv[0, :, where]
        s = jnp.dot(qs[h], jnp.concatenate([keys, keys], axis=0), preferred_element_type=F32)
        s_ref[:, : where.size] = s
        before = m_s[h]
        peak = jnp.maximum(before, jnp.max(s, axis=1, keepdims=True))
        m_s[h] = peak
        peak_ref[...] = peak
        factor_ref[...] = jnp.exp2(before - peak)

    def mix(h, where, held):
        s_ref, peak_ref, factor_ref = held
        peak, factor = peak_ref[...], factor_ref[...]
        probs, total = [], None
        for g in range(where.size // HEAD):
            p = jnp.exp2(s_ref[:, g * HEAD : (g + 1) * HEAD] - peak)
            total = p if total is None else total + p
            probs.append(p.astype(BF16))
        mixed = jnp.dot(jnp.concatenate(probs, axis=1), vn[where, :], preferred_element_type=F32)
        l_s[h] = l_s[h] * factor + total
        acc_s[h] = acc_s[h] * factor + mixed

    def pipelined(first, last, block, count):
        where = pl.ds(pl.multiple_of(block * SEQ, SEQ), count * SEQ)
        even, odd = (s_even, p_even, f_even), (s_odd, p_odd, f_odd)
        scores(first, where, even)

        def body(i, carry):
            h = 2 * i
            scores(h + 1, where, odd)
            mix(h, where, even)
            scores(h + 2, where, even)
            mix(h + 1, where, odd)
            return carry

        lax.fori_loop(first // 2, last // 2 - 1, body, 0)
        scores(last - 1, where, odd)
        mix(last - 2, where, even)
        mix(last - 1, where, odd)

    own_heads = jnp.where(donor, HEADS - HELP, HEADS)

    def take(block):
        @pl.when(needs(me, block))
        def _():
            push(block, me).wait_recv()
            forward(block).start()

    forward(me).wait_recv()
    turn(me)
    heads(0, own_heads, me, 1, diagonal=True)

    others(lambda other: ask(other, other).wait_recv())
    load_k.wait()
    load_v.wait()

    def decode_head(g):
        columns = pl.ds(pl.multiple_of(g * HEAD, HEAD), HEAD)
        mine, next_ = drecv[2 * g], drecv[2 * g + 1]
        q = jnp.concatenate([mine[:32], next_[:32]], axis=0)
        a, b = mine[32:48].astype(F32)[:8], next_[32:48].astype(F32)[:8]
        left = lane < 64
        new_k = jnp.where(left, a, pltpu.roll(b, 64, 1))
        new_v = jnp.where(left, pltpu.roll(a, 64, 1), b)
        new_k = jnp.where(first_rows, new_k, pltpu.roll(new_k, 4, 0))
        new_v = jnp.where(first_rows, new_v, pltpu.roll(new_v, 4, 0))
        s = lax.dot_general(
            q, kpool[:, columns], (((1,), (1,)), ((), ())), preferred_element_type=F32
        )
        s = (s * SCALE).reshape(8, 8, SPAN) + bias[...][None]
        own = jnp.sum(q.astype(F32).reshape(8, 8, HEAD) * new_k[None], axis=2, keepdims=True)
        own = own * SCALE
        peak = jnp.maximum(jnp.max(s, axis=2, keepdims=True), own)
        p = jnp.exp2(s - peak)
        own = jnp.exp2(own - peak)
        total = jnp.sum(p, axis=2, keepdims=True) + own
        mixed = jnp.dot(
            p.reshape(64, SPAN).astype(BF16), vpool[:, columns], preferred_element_type=F32
        ).reshape(8, 8, HEAD)
        mixed = mixed + own.astype(BF16).astype(F32) * new_v[None]
        result = (mixed / total).reshape(64, HEAD).astype(BF16)
        rsend[2 * g] = result[:32]
        rsend[2 * g + 1] = result[32:]

    def decode_two(i, carry):
        decode_head(2 * i)
        decode_head(2 * i + 1)
        return carry

    lax.fori_loop(0, GROUPS // 2, decode_two, 0)
    rrecv[tp] = rsend[tp]
    others(lambda other: answer(other, tp).start())

    for d in (1, 2, 3):
        take(me ^ d)

    def full(block):
        @pl.when(needs(me, block))
        def _():
            forward(block).wait_recv()
            turn(block)

    full(me ^ 1)

    @pl.when(me % 2 == 1)
    def _():
        heads(0, own_heads, me - 1, 1)

    full(me ^ 2)
    full(me ^ 3)
    for d in (6, 7, 4, 5):
        take(me ^ d)

    @pl.when(me // 2 % 2 == 1)
    def _():
        pipelined(0, own_heads, me // 4 * 4, 2)

    for d in (6, 7, 4, 5):
        full(me ^ d)

    @pl.when(helper)
    def _():
        for i in range(HELP):
            lend(i).wait_recv()
            qs[HEADS + i] = split_scaled(lent[i])
        heads(HEADS, HEADS + HELP, partner, 1, diagonal=True)
        heads(HEADS, HEADS + HELP, 0, 4)
        heads(HEADS, HEADS + HELP, 4, 2)

        @pl.when(me == 1)
        def _():
            heads(HEADS, HEADS + HELP, 6, 1)

        for i in range(HELP):
            total = jnp.sum(l_s[HEADS + i], axis=1, keepdims=True)
            repaid[i] = (acc_s[HEADS + i] / total).astype(BF16)
            give_back(i).start()

    @pl.when(me // 4 == 1)
    def _():
        pipelined(0, own_heads, 0, 4)

    def normalise(h):
        total = jnp.sum(l_s[h], axis=1, keepdims=True)
        out_ref[:, h * HEAD : (h + 1) * HEAD] = (acc_s[h] / total).astype(BF16)

    for h in range(HEADS - HELP):
        normalise(h)

    @pl.when(jnp.logical_not(donor))
    def _():
        for h in range(HEADS - HELP, HEADS):
            normalise(h)

    for d in nearest:

        @pl.when(jnp.logical_not(needs(me, me ^ d)))
        def _(d=d):
            push(me ^ d, me).wait_recv()

    def relay(which, result):
        def body(p, carry):
            rows = pl.ds(pl.multiple_of(core * 64 + p * 16, 16), 16)
            slots = [jnp.zeros((16, PAGE), BF16)] * 4
            for b in range(CTX * 4):
                block = kv[which, rows, b * PAGE : (b + 1) * PAGE]
                for i in range(4):
                    chosen = jnp.where(place_ref[b] == me * 4 + i, 1.0, 0.0)
                    slots[i] = slots[i] + block * jnp.full((16, PAGE), chosen, F32).astype(BF16)
            for i in range(4):
                result[i, pl.ds(pl.multiple_of(p * 16, 16), 16), :] = slots[i]
            return carry

        lax.fori_loop(0, 4, body, 0)

    relay(0, rk_ref)
    relay(1, rv_ref)

    others(lambda other: answer(other, other).wait_recv())
    for p in range(4):
        pieces = []
        for o in range(2):
            even = rrecv[4 * p + 2 * o].astype(F32)
            odd = rrecv[4 * p + 2 * o + 1].astype(F32)
            columns = []
            for i in range(4):
                a, b = even[8 * i : 8 * i + 8], odd[8 * i : 8 * i + 8]
                columns.append(jnp.where(first_rows, a, pltpu.roll(b, 4, 0)))
                columns.append(jnp.where(first_rows, pltpu.roll(a, 4, 0), b))
            pieces.append(jnp.concatenate(columns, axis=1))
        dout_ref[16 * p : 16 * p + 16, :] = jnp.concatenate(pieces, axis=0).astype(BF16)

    @pl.when(donor)
    def _():
        for i in range(HELP):
            give_back(i).wait_recv()
            h = HEADS - HELP + i
            out_ref[:, h * HEAD : (h + 1) * HEAD] = returned[i]
            lend(i).wait_send()

    @pl.when(helper)
    def _():
        for i in range(HELP):
            give_back(i).wait_send()

    forward(me).wait_send()
    for d in range(1, CTX):
        push(me, me ^ d).wait_send()

        @pl.when(needs(me, me ^ d))
        def _(d=d):
            forward(me ^ d).wait_send()

    others(lambda other: ask(other, tp).wait_send())
    others(lambda other: answer(other, tp).wait_send())


def finish(*refs):
    count = (len(refs) - 1) // 2
    copies = [
        pltpu.make_async_copy(refs[i], refs[count + i], refs[-1].at[i]) for i in range(count)
    ]
    for copy in copies:
        copy.start()
    for copy in copies:
        copy.wait()


def shards(
    prompt_queries,
    prompt_keys,
    prompt_values,
    block_slot,
    decode_queries,
    new_keys,
    new_values,
    key_pool,
    value_pool,
    slot_map,
    cache_lengths,
):
    vmem = pl.BlockSpec(memory_space=pltpu.VMEM)
    smem = pl.BlockSpec(memory_space=pltpu.SMEM)
    hbm = pl.BlockSpec(memory_space=pl.ANY)
    state = pltpu.VMEM((HEADS + HELP, SEQ, HEAD), F32)
    dma = pltpu.SemaphoreType.DMA
    shapes = (
        jax.ShapeDtypeStruct((SEQ, HEADS * HEAD), BF16),
        jax.ShapeDtypeStruct((4, 64, PAGE), BF16),
        jax.ShapeDtypeStruct((4, 64, PAGE), BF16),
        jax.ShapeDtypeStruct((64, HEADS * HEAD), BF16),
    )
    results = pl.pallas_call(
        kernel,
        out_shape=tuple(pltpu.VMEM(one.shape, one.dtype) for one in shapes),
        in_specs=[hbm, hbm, hbm, hbm, hbm, hbm, hbm, hbm, smem, smem, smem],
        out_specs=(vmem, vmem, vmem, vmem),
        scratch_shapes=[
            pltpu.VMEM((SEQ, HEADS * HEAD), BF16),
            pltpu.VMEM((HEADS + HELP, SEQ, 2 * HEAD), BF16),
            pltpu.VMEM((2, HEAD, CTX * SEQ), BF16),
            pltpu.VMEM((CTX * SEQ, HEAD), BF16),
            state,
            state,
            state,
            pltpu.VMEM((SPAN, GROUPS * HEAD), BF16),
            pltpu.VMEM((SPAN, GROUPS * HEAD), BF16),
            pltpu.VMEM((8, SPAN), F32),
            pltpu.VMEM((TP, MSG, HEAD), BF16),
            pltpu.VMEM((TP, MSG, HEAD), BF16),
            pltpu.VMEM((TP, 32, HEAD), BF16),
            pltpu.VMEM((TP, 32, HEAD), BF16),
            pltpu.VMEM((HELP, SEQ, HEAD), BF16),
            pltpu.VMEM((HELP, SEQ, HEAD), BF16),
            pltpu.VMEM((HELP, SEQ, HEAD), BF16),
            pltpu.VMEM((SEQ, 4 * SEQ), F32),
            pltpu.VMEM((SEQ, 4 * SEQ), F32),
            pltpu.VMEM((SEQ, HEAD), F32),
            pltpu.VMEM((SEQ, HEAD), F32),
            pltpu.VMEM((SEQ, HEAD), F32),
            pltpu.VMEM((SEQ, HEAD), F32),
            pltpu.VMEM((64, SEQ), BF16),
            pltpu.VMEM((64, SEQ), BF16),
            pltpu.VMEM((64, HEADS * HEAD), BF16),
            pltpu.VMEM((64, 64), BF16),
            pltpu.VMEM((64, 64), BF16),
            dma((8,)),
            dma((CTX,)),
            dma((CTX,)),
            dma((CTX,)),
            dma((CTX,)),
            dma((TP,)),
            dma((TP,)),
            dma((TP,)),
            dma((TP,)),
            dma((HELP,)),
            dma((HELP,)),
            dma((HELP,)),
            dma((HELP,)),
        ],
        compiler_params=pltpu.CompilerParams(
            collective_id=0, has_side_effects=True, vmem_limit_bytes=56 * 2**20
        ),
    )(
        prompt_queries,
        prompt_keys.T,
        prompt_values.T,
        decode_queries,
        new_keys,
        new_values,
        key_pool.reshape(SPAN, GROUPS * HEAD),
        value_pool.reshape(SPAN, GROUPS * HEAD),
        slot_map,
        cache_lengths,
        block_slot,
    )
    prompt_out, relaid_keys, relaid_values, decode_out = pl.pallas_call(
        finish,
        out_shape=shapes,
        in_specs=[vmem] * 4,
        out_specs=(hbm,) * 4,
        scratch_shapes=[dma((4,))],
    )(*[pltpu.with_memory_space_constraint(one, pltpu.VMEM) for one in results])
    return (
        prompt_out,
        jnp.swapaxes(relaid_keys, 1, 2),
        jnp.swapaxes(relaid_values, 1, 2),
        decode_out,
    )


def solution(mesh):
    return jax.shard_map(
        shards,
        mesh=mesh,
        in_specs=(
            P("ctx", "tp"),
            P("ctx", "tp"),
            P("ctx", "tp"),
            P(),
            P("ctx", "tp"),
            P("ctx", "tp"),
            P("ctx", "tp"),
            P(("ctx", "tp"), None, None),
            P(("ctx", "tp"), None, None),
            P(("ctx", "tp"), None),
            P(("ctx", "tp")),
        ),
        out_specs=(P("ctx", "tp"), P("ctx", None, "tp"), P("ctx", None, "tp"), P("ctx", "tp")),
        check_vma=False,
    )
```

profile of v0, /device:TPU:0, one launch (start us, length us, event | category | flops | bytes accessed | tf_op | source)
XLA Modules:
  0.0 40.9 jit_solution(412201473936803232)
XLA Ops:
  0.6 39.0 %shard_map.138 = (bf16[512,1024]{1,0:T(8,128)(2,1)S(1)}, bf16[4,64,128]{2,1,0:T(8,128)(2,1)S(1)}, bf16[4,64,128]{2,1,0:T(8,128)(2,1)S(1)}, bf16[64,1024]{1,0:T(8,128)(2,1)S(1)}) custom-call(bf16[512,1024]{1,0:T(8,128)(2,1)} %pq_ref.1, bf16[64,512]{1,0:T(8,128)(2,1)} %bitcast.8, bf16[64,512]{1,0:T(8,128)(2,1)} %bitcast.9, bf16[64,1024]{1,0:T(8,128)(2,1)} %dq_in.1, ...), custom_call_target="tpu_custom_call" | custom-call | tf_op jit(solution)/shard_map/pallas_call | solution.py:506
  39.6 1.1 %shard_map.139 = (bf16[512,1024]{1,0:T(8,128)(2,1)}, bf16[4,64,128]{2,1,0:T(8,128)(2,1)}, bf16[4,64,128]{2,1,0:T(8,128)(2,1)}, bf16[64,1024]{1,0:T(8,128)(2,1)}) custom-call(bf16[512,1024]{1,0:T(8,128)(2,1)S(1)} %get-tuple-element.12.refs_0_, bf16[4,64,128]{2,1,0:T(8,128)(2,1)S(1)} %get-tuple-element.13.refs_1_, ...), custom_call_target="tpu_custom_call" | custom-call | tf_op jit(solution)/shard_map/pallas_call | solution.py:570
where the time goes:
time: 41.6 us; the launch traced here: 40.9 us
  Pallas kernels  40.1 us (96%)
  between operations  0.82 us (2%)
    pallas_call x1, Pallas kernels, shards(): pl.pallas_call(kernel, out_shape=tuple((pltpu.VMEM(one.shape, one.dtype)...  39 us
    pallas_call x1, Pallas kernels, shards(): pl.pallas_call(finish, out_shape=shapes, in_specs=[vmem] * 4, out_specs=(...  1.08 us

commit v1 on v0

--- a/solution.py
+++ b/solution.py
@@ -376,18 +376,23 @@
         for i in range(HELP):
             lend(i).wait_recv()
             qs[HEADS + i] = split_scaled(lent[i])
-        heads(HEADS, HEADS + HELP, partner, 1, diagonal=True)
-        heads(HEADS, HEADS + HELP, 0, 4)
-        heads(HEADS, HEADS + HELP, 4, 2)
-
-        @pl.when(me == 1)
-        def _():
-            heads(HEADS, HEADS + HELP, 6, 1)
-
-        for i in range(HELP):
-            total = jnp.sum(l_s[HEADS + i], axis=1, keepdims=True)
-            repaid[i] = (acc_s[HEADS + i] / total).astype(BF16)
+
+        def help_with(i, carry):
+            h = HEADS + i
+            unit(h, partner, 1, True)
+            unit(h, 0, 4, False)
+            unit(h, 4, 2, False)
+
+            @pl.when(me == 1)
+            def _():
+                unit(h, 6, 1, False)
+
+            total = jnp.sum(l_s[h], axis=1, keepdims=True)
+            repaid[i] = (acc_s[h] / total).astype(BF16)
             give_back(i).start()
+            return carry
+
+        lax.fori_loop(0, HELP, help_with, 0)
 
     @pl.when(me // 4 == 1)
     def _():

time: 41.6 us -> 40.6 us (0.976)
  the two profiles are of different devices: /device:TPU:0 before, /device:TPU:96 now
where the time goes in v1:
time: 40.6 us; the launch traced here: 40.5 us
  Pallas kernels  39.7 us (98%)
  between operations  0.82 us (2%)
    pallas_call x1, Pallas kernels, shards(): pl.pallas_call(kernel, out_shape=tuple((pltpu.VMEM(one.shape, one.dtype)...  38.6 us
    pallas_call x1, Pallas kernels, shards(): pl.pallas_call(finish, out_shape=shapes, in_specs=[vmem] * 4, out_specs=(...  1.08 us

profile of v1, /device:TPU:96, one launch (start us, length us, event | category | flops | bytes accessed | tf_op | source)
XLA Modules:
  0.0 40.5 jit_solution(11782116411286748517)
XLA Ops:
  0.6 38.6 %shard_map.138 = (bf16[512,1024]{1,0:T(8,128)(2,1)S(1)}, bf16[4,64,128]{2,1,0:T(8,128)(2,1)S(1)}, bf16[4,64,128]{2,1,0:T(8,128)(2,1)S(1)}, bf16[64,1024]{1,0:T(8,128)(2,1)S(1)}) custom-call(bf16[512,1024]{1,0:T(8,128)(2,1)} %pq_ref.1, bf16[64,512]{1,0:T(8,128)(2,1)} %bitcast.8, bf16[64,512]{1,0:T(8,128)(2,1)} %bitcast.9, bf16[64,1024]{1,0:T(8,128)(2,1)} %dq_in.1, ...), custom_call_target="tpu_custom_call" | custom-call | tf_op jit(solution)/shard_map/pallas_call | solution.py:511
  39.2 1.1 %shard_map.139 = (bf16[512,1024]{1,0:T(8,128)(2,1)}, bf16[4,64,128]{2,1,0:T(8,128)(2,1)}, bf16[4,64,128]{2,1,0:T(8,128)(2,1)}, bf16[64,1024]{1,0:T(8,128)(2,1)}) custom-call(bf16[512,1024]{1,0:T(8,128)(2,1)S(1)} %get-tuple-element.12.refs_0_, bf16[4,64,128]{2,1,0:T(8,128)(2,1)S(1)} %get-tuple-element.13.refs_1_, ...), custom_call_target="tpu_custom_call" | custom-call | tf_op jit(solution)/shard_map/pallas_call | solution.py:575
